TPU v7x, 128 devices: a whole 4x4x4 slice. The times are simulated.
128 devices in a mesh: seq: 32 (over x, z, y_lo), tp: 4 (over y_hi, core).
Axes of the slice: x: 4, y: 4 (y_hi: 2, y_lo: 2; y = y_hi * 2 + y_lo), z: 4, core: 2. Of those that a mesh axis runs over, the one named last changes fastest.
Arguments:
- context: bfloat16 [65536, 2048], P('seq'), may hold values from -40 to 40
- latent_in: bfloat16 [1024, 2048], P('seq'), may hold values from -24 to 24
- cutoff: int32 [1024], replicated, may hold values from 0 to 65535, as said below
- wq_cross: bfloat16 [2048, 2048], P(None, 'tp'), may hold values from -0.6 to 0.6
- wk_cross: bfloat16 [2048, 2048], P(None, 'tp'), may hold values from -0.6 to 0.6
- wv_cross: bfloat16 [2048, 2048], P(None, 'tp'), may hold values from -0.125 to 0.125
- wo_cross: bfloat16 [2048, 2048], P('tp'), may hold values from -0.125 to 0.125
- wq_self: bfloat16 [2048, 2048], P(None, 'tp'), may hold values from -0.6 to 0.6
- wk_self: bfloat16 [2048, 2048], P(None, 'tp'), may hold values from -0.6 to 0.6
- wv_self: bfloat16 [2048, 2048], P(None, 'tp'), may hold values from -0.125 to 0.125
- wo_self: bfloat16 [2048, 2048], P('tp'), may hold values from -0.125 to 0.125
Outputs:
- latent_out: bfloat16 [1024, 2048], P('seq')
Inputs may be any that keep to these rules, and one draw needn't show every extreme that they name: `cutoff`: strictly increasing; the last entry is 65535.
All inputs are finite; a program needn't handle non-finite values.
Results may differ from a plain program's by a relative error of at most 0.012.
Values may be sent and summed in bfloat16 or wider, within the bound.
No kernel may reach another device: no remote copies, remote signals or barrier semaphores. Data moves between devices by JAX's collectives and lax.ppermute only.
A program may use at most 192 MiB of HBM per device.

v0:
```python
import functools

import jax
import jax.numpy as jnp
from jax import lax
from jax.experimental import pallas as pl
from jax.experimental.pallas import tpu as pltpu
from jax.sharding import Mesh, PartitionSpec as P

HEAD_DIM = 128
EPSILON = 1e-05
MASKED_SCORE = -1e30
LOG2E = 1.4426950408889634
MIB = 1 << 20
F32 = jnp.float32
BF16 = jnp.bfloat16

VMEM = pl.BlockSpec(memory_space=pltpu.VMEM)
SMEM = pl.BlockSpec(memory_space=pltpu.SMEM)


def shape_of(dims, dtype=BF16):
    return jax.ShapeDtypeStruct(dims, dtype)


def params(mib):
    return pltpu.CompilerParams(vmem_limit_bytes=mib * MIB)


def cost(flops, nbytes, trans=0):
    return pl.CostEstimate(flops=flops, bytes_accessed=nbytes, transcendentals=trans)


def dot(a, b):
    return jnp.dot(a, b, preferred_element_type=F32)


def dot_t(a, b):
    return lax.dot_general(a, b, (((1,), (1,)), ((), ())), preferred_element_type=F32)


def inv_rms(tile):
    return lax.rsqrt(jnp.mean(tile * tile, axis=-1, keepdims=True) + EPSILON)


def query_kernel(latent_ref, wq_ref, out_ref):
    tile = latent_ref[...].astype(F32)
    normed = (tile * inv_rms(tile)).astype(BF16)
    factor = HEAD_DIM ** (-0.5) * LOG2E
    out_ref[...] = (dot(normed, wq_ref[...]) * factor).astype(BF16)


def project_queries(latent_in, wq):
    rows, width = latent_in.shape
    cols = wq.shape[1]
    return pl.pallas_call(
        query_kernel,
        out_shape=shape_of((rows, cols)),
        in_specs=[VMEM, VMEM],
        out_specs=VMEM,
        compiler_params=params(8),
        cost_estimate=cost(2 * rows * width * cols, 2 * width * cols),
        name="queries",
    )(latent_in, wq)


def context_kernel(step, context_ref, w_ref, after_ref, out_ref):
    def rows_from(i, _):
        here = pl.ds(pl.multiple_of(i * step, step), step)
        tile = context_ref[here, :]
        out_ref[here, :] = (dot(tile, w_ref[...]) * inv_rms(tile.astype(F32))).astype(BF16)
        return 0

    lax.fori_loop(0, context_ref.shape[0] // step, rows_from, 0)


def project_context(context, weight, after, name):
    rows, width = context.shape
    cols = weight.shape[1]
    return pl.pallas_call(
        functools.partial(context_kernel, min(512, rows)),
        out_shape=shape_of((rows, cols)),
        in_specs=[VMEM, VMEM, pl.BlockSpec(memory_space=pl.ANY)],
        out_specs=VMEM,
        compiler_params=params(20),
        cost_estimate=cost(2 * rows * width * cols, 2 * (rows * width + width * cols)),
        name=name,
    )(context, weight, after)


def packed_totals(totals):
    lane = lax.broadcasted_iota(jnp.int32, totals[0].shape, 1)
    held = jnp.zeros(totals[0].shape, F32)
    for head, total in enumerate(totals):
        held = jnp.where(lane == head, total, held)
    high = held.astype(BF16).astype(F32)
    rest = held - high
    mid = rest.astype(BF16).astype(F32)
    low = rest - mid
    return (high + pltpu.roll(mid, 4, 1) + pltpu.roll(low, 8, 1)).astype(BF16)


def spread_matrix(heads):
    dims = (HEAD_DIM, heads * HEAD_DIM)
    row = lax.broadcasted_iota(jnp.int32, dims, 0)
    head = lax.broadcasted_iota(jnp.int32, dims, 1) >> 7
    return jnp.where((row < 12) & ((row & 3) == head), 1.0, 0.0).astype(BF16)


def cross_kernel(offset, ids_ref, cutoff_ref, q_ref, k_ref, v_ref, cut_ref, out_ref, bias):
    rows, cols = q_ref.shape
    heads = cols // HEAD_DIM
    places = k_ref.shape[0]
    step = 512
    block = lax.rem(ids_ref[0] + offset, 4)
    start = block * rows
    first_pos = ids_ref[2]
    lowest = cutoff_ref[start] - first_pos
    highest = cutoff_ref[start + rows - 1] - first_pos
    spans = [slice(head * HEAD_DIM, (head + 1) * HEAD_DIM) for head in range(heads)]

    @pl.when(highest < 0)
    def _():
        out_ref[:, :cols] = jnp.zeros((rows, cols), BF16)
        out_ref[:, cols:] = packed_totals(
            [jnp.full((rows, HEAD_DIM), MASKED_SCORE, F32)] * heads
        )

    def attend(masked):
        ones = jnp.ones((step, HEAD_DIM), BF16)
        if masked:
            cut = cut_ref[pl.ds(pl.multiple_of(start, rows), rows), :] - first_pos
            order = lax.broadcasted_iota(jnp.int32, (rows, HEAD_DIM), 1)
            for place in range(0, places, HEAD_DIM):
                bias[:, place : place + HEAD_DIM] = jnp.where(
                    order + place <= cut, 0.0, MASKED_SCORE
                )

        def scores_of(head):
            scores = dot_t(q_ref[:, spans[head]], k_ref[:, spans[head]])
            return scores + bias[...] if masked else scores

        totals = []
        scores = scores_of(0)
        for head in range(heads):
            peak = jnp.max(scores, axis=1, keepdims=True)
            later = scores_of(head + 1) if head + 1 < heads else None
            both = jnp.zeros((rows, 2 * HEAD_DIM), F32)
            for place in range(0, places, step):
                here = slice(place, place + step)
                probs = jnp.exp2(scores[:, here] - peak).astype(BF16)
                both += dot(probs, jnp.concatenate([v_ref[here, spans[head]], ones], axis=1))
            total = both[:, HEAD_DIM:]
            out_ref[:, spans[head]] = (both[:, :HEAD_DIM] / total).astype(BF16)
            whole = jnp.log2(total) + peak
            totals.append(jnp.where(cut >= 0, whole, MASKED_SCORE) if masked else whole)
            scores = later
        out_ref[:, cols:] = packed_totals(totals)

    @pl.when((highest >= 0) & (lowest < places - 1))
    def _():
        attend(True)

    @pl.when(lowest >= places - 1)
    def _():
        attend(False)


def cross_attend(offset, ids, cutoff, queries, keys, values, cut_wide):
    rows, cols = queries.shape
    places = keys.shape[0]
    return pl.pallas_call(
        functools.partial(cross_kernel, offset),
        out_shape=shape_of((rows, cols + HEAD_DIM)),
        in_specs=[SMEM, SMEM, VMEM, VMEM, VMEM, VMEM],
        out_specs=VMEM,
        scratch_shapes=[pltpu.VMEM((rows, places), F32)],
        compiler_params=params(20),
        cost_estimate=cost(8 * rows * places * cols, 4 * places * cols, rows * places * 4),
        name="cross",
    )(ids, cutoff, queries, keys, values, cut_wide)


def blend(parts, spread, heads):
    cols = heads * HEAD_DIM
    totals = [dot(part[:, cols:], spread) for part in parts]
    peak = functools.reduce(jnp.maximum, totals)
    weights = [jnp.exp2(total - peak) for total in totals]
    weight_sum = functools.reduce(jnp.add, weights)
    mixed = functools.reduce(
        jnp.add, [w * part[:, :cols].astype(F32) for w, part in zip(weights, parts)]
    )
    return mixed / weight_sum, peak + jnp.log2(weight_sum)


def blend_kernel(a_ref, b_ref, c_ref, d_ref, out_ref):
    rows, width = a_ref.shape
    heads = width // HEAD_DIM - 1
    cols = heads * HEAD_DIM
    mixed, whole = blend(
        [a_ref[...], b_ref[...], c_ref[...], d_ref[...]], spread_matrix(heads), heads
    )
    out_ref[:, :cols] = mixed.astype(BF16)
    out_ref[:, cols:] = packed_totals(
        [whole[:, head * HEAD_DIM : (head + 1) * HEAD_DIM] for head in range(heads)]
    )


def blend_parts(parts):
    return pl.pallas_call(
        blend_kernel,
        out_shape=shape_of(parts[0].shape),
        in_specs=[VMEM] * 4,
        out_specs=VMEM,
        compiler_params=params(16),
        name="blend",
    )(*parts)


def cross_output_kernel(parts_ref, wo_ref, out_ref):
    heads = parts_ref.shape[2] // HEAD_DIM - 1
    parts = [parts_ref[i] for i in range(parts_ref.shape[0])]
    mixed, _ = blend(parts, spread_matrix(heads), heads)
    out_ref[...] = dot(mixed.astype(BF16), wo_ref[...]).astype(BF16)


def cross_output(parts, wo):
    return pl.pallas_call(
        cross_output_kernel,
        out_shape=shape_of((parts.shape[1], wo.shape[1])),
        in_specs=[VMEM] * 2,
        out_specs=VMEM,
        compiler_params=params(16),
        name="cross_output",
    )(parts, wo)


def self_project_kernel(
    ids_ref, latent_ref, one_ref, two_ref, wq_ref, wk_ref, wv_ref, state_ref, *rest
):
    outs, held = rest[:4], rest[4]
    rows, cols = held.shape[1:]
    state = latent_ref[...].astype(F32) + (one_ref[...].astype(F32) + two_ref[...].astype(F32))
    state_ref[...] = state
    normed = (state * inv_rms(state)).astype(BF16)
    held[0] = (dot(normed, wq_ref[...]) * (HEAD_DIM ** (-0.5) * LOG2E)).astype(BF16)
    held[1] = dot(normed, wk_ref[...]).astype(BF16)
    held[2] = dot(normed, wv_ref[...]).astype(BF16)
    for offset in range(4):
        head = lax.rem(ids_ref[0] + offset, 4)
        span = pl.ds(pl.multiple_of(head * HEAD_DIM, HEAD_DIM), HEAD_DIM)
        for part in range(3):
            outs[offset][:, part * HEAD_DIM : (part + 1) * HEAD_DIM] = held[part, :, span]


def self_project(ids, latent_in, one, two, wq, wk, wv):
    rows, width = latent_in.shape
    return pl.pallas_call(
        self_project_kernel,
        out_shape=[shape_of((rows, width), F32)] + [shape_of((rows, 3 * HEAD_DIM))] * 4,
        in_specs=[SMEM] + [VMEM] * 6,
        out_specs=[VMEM] * 5,
        scratch_shapes=[pltpu.VMEM((3, rows, wq.shape[1]), BF16)],
        compiler_params=params(24),
        name="self_project",
    )(ids, latent_in, one, two, wq, wk, wv)


def self_kernel(ids_ref, a_ref, b_ref, c_ref, d_ref, kv_ref, *outs):
    rows = a_ref.shape[0]
    groups, group_rows, _ = kv_ref.shape
    own_x, own_zy = ids_ref[0], ids_ref[1]
    q = jnp.concatenate([ref[:, :HEAD_DIM] for ref in (a_ref, b_ref, c_ref, d_ref)], axis=0)
    k = jnp.concatenate([kv_ref[i, :, :HEAD_DIM] for i in range(groups)], axis=0)
    v = jnp.concatenate([kv_ref[i, :, HEAD_DIM:] for i in range(groups)], axis=0)
    scores = dot_t(q, k)
    q_row = lax.broadcasted_iota(jnp.int32, scores.shape, 0)
    k_row = lax.broadcasted_iota(jnp.int32, scores.shape, 1)
    shift = rows.bit_length() - 1
    q_x = (own_x - (q_row >> shift)) & 3
    q_place = (q_x * groups + own_zy) * rows + (q_row & (rows - 1))
    group = k_row >> (group_rows.bit_length() - 1)
    k_x = (own_x - (k_row >> shift)) & 3
    k_place = (k_x * groups + group) * rows + (k_row & (rows - 1))
    scores = jnp.where(k_place <= q_place, scores, MASKED_SCORE)
    peak = jnp.max(scores, axis=1, keepdims=True)
    probs = jnp.exp2(scores - peak).astype(BF16)
    both = dot(probs, jnp.concatenate([v, jnp.ones(v.shape, BF16)], axis=1))
    result = (both[:, :HEAD_DIM] / both[:, HEAD_DIM:]).astype(BF16)
    for offset in range(4):
        outs[offset][...] = result[offset * rows : (offset + 1) * rows]


def self_attend(ids, parts, kv):
    rows = parts[0].shape[0]
    return pl.pallas_call(
        self_kernel,
        out_shape=[shape_of((rows, HEAD_DIM))] * 4,
        in_specs=[SMEM] + [VMEM] * 5,
        out_specs=[VMEM] * 4,
        compiler_params=params(16),
        name="self_attend",
    )(ids, *parts, kv)


def self_output_kernel(ids_ref, a_ref, b_ref, c_ref, d_ref, wo_ref, out_ref, held):
    for offset, ref in enumerate((a_ref, b_ref, c_ref, d_ref)):
        head = lax.rem(ids_ref[0] + offset, 4)
        held[:, pl.ds(pl.multiple_of(head * HEAD_DIM, HEAD_DIM), HEAD_DIM)] = ref[...]
    out_ref[...] = dot(held[...], wo_ref[...]).astype(BF16)


def self_output(ids, parts, wo):
    rows = parts[0].shape[0]
    return pl.pallas_call(
        self_output_kernel,
        out_shape=shape_of((rows, wo.shape[1])),
        in_specs=[SMEM] + [VMEM] * 5,
        out_specs=VMEM,
        scratch_shapes=[pltpu.VMEM((rows, wo.shape[0]), BF16)],
        compiler_params=params(16),
        name="self_output",
    )(ids, *parts, wo)


def moved(tensor, axis, size, offset):
    return lax.ppermute(tensor, axis, [(i, (i + offset) % size) for i in range(size)])


def summed_over_tp(part):
    other = moved(part, "core", 2, 1)
    pair = (part.astype(F32) + other.astype(F32)).astype(BF16)
    return pair, moved(pair, "y_hi", 2, 1)


def on_device(
    context,
    latent_in,
    cutoff,
    wq_cross,
    wk_cross,
    wv_cross,
    wo_cross,
    wq_self,
    wk_self,
    wv_self,
    wo_self,
):
    x = lax.axis_index("x")
    zy = lax.axis_index("z") * 2 + lax.axis_index("y_lo")
    ids = jnp.stack([x, zy, (x * 8 + zy) * context.shape[0]]).astype(jnp.int32)
    cut_wide = jnp.broadcast_to(cutoff[:, None], (cutoff.shape[0], HEAD_DIM))

    own = project_queries(latent_in, wq_cross)
    other = moved(own, "y_lo", 2, 1)
    y_lo = lax.axis_index("y_lo")
    pair = jnp.where(
        y_lo == 0, jnp.concatenate([own, other]), jnp.concatenate([other, own])
    )
    keys = project_context(context, wk_cross, pair, "keys")
    z = lax.axis_index("z")
    ring = [pair] + [moved(pair, "z", 4, offset) for offset in (1, 2, 3)]
    pieces = [
        lax.dynamic_index_in_dim(jnp.stack(ring), (z - place) % 4, 0, False) for place in range(4)
    ]
    mine = jnp.concatenate(pieces)
    values = project_context(context, wv_cross, mine, "values")
    blocks = {0: mine}
    for offset in (2, 3, 1):
        blocks[(4 - offset) % 4] = moved(mine, "x", 4, offset)

    parts = []
    for offset in (0, 1, 2, 3):
        part = cross_attend(offset, ids, cutoff, blocks[offset], keys, values, cut_wide)
        parts.append(moved(part, "x", 4, offset) if offset else part)
    mixed = blend_parts(parts)
    rows = latent_in.shape[0]
    mixed = mixed.reshape(8, rows, mixed.shape[1])
    mixed = lax.all_to_all(mixed, ("z", "y_lo"), 0, 0)
    cross_part = cross_output(mixed, wo_cross)
    one, two = summed_over_tp(cross_part)

    state, *sent = self_project(ids, latent_in, one, two, wq_self, wk_self, wv_self)
    parts = [sent[0]] + [moved(sent[o], "x", 4, o) for o in (1, 2, 3)]
    kv = jnp.concatenate([part[:, HEAD_DIM:] for part in parts])
    kv = lax.all_to_all(jnp.broadcast_to(kv[None], (8,) + kv.shape), ("z", "y_lo"), 0, 0)
    outs = self_attend(ids, parts, kv)
    outs = [outs[0]] + [moved(outs[o], "x", 4, -o) for o in (1, 2, 3)]
    self_part = self_output(ids, outs, wo_self)
    one, two = summed_over_tp(self_part)
    return (state + (one.astype(F32) + two.astype(F32))).astype(BF16)


def solution(mesh):
    fine = Mesh(
        mesh.devices.reshape(4, 4, 2, 2, 2), ("x", "z", "y_lo", "y_hi", "core")
    )
    seq, tp = ("x", "z", "y_lo"), ("y_hi", "core")
    in_specs = (
        P(seq, None),
        P(seq, None),
        P(),
        P(None, tp),
        P(None, tp),
        P(None, tp),
        P(tp, None),
        P(None, tp),
        P(None, tp),
        P(None, tp),
        P(tp, None),
    )
    return jax.shard_map(
        on_device, mesh=fine, in_specs=in_specs, out_specs=P(seq, None), check_vma=False
    )
```

profile of v0, /device:TPU:1, one launch (start us, length us, event | category | flops | bytes accessed | tf_op | source)
XLA Modules:
  0.0 122.7 jit_solution(1762764251340666010)
XLA Ops:
  0.0 1.6 %copy-done.2 = bf16[2048,512]{1,0:T(8,128)(2,1)S(1)} copy-done((bf16[2048,512]{1,0:T(8,128)(2,1)S(1)}, bf16[2048,512]{1,0:T(8,128)(2,1)}, u32[]{:S(2)}) %copy-start.2) | copy-done | bytes 2097176
  1.6 0.9 copy-done.6
  2.5 0.5 queries.1
  3.0 2.2 %collective-permute-start = (bf16[32,512]{1,0:T(8,128)(2,1)S(1)}, bf16[32,512]{1,0:T(8,128)(2,1)S(1)}, u32[]{:S(2)}, u32[]{:S(2)}) collective-permute-start(bf16[32,512]{1,0:T(8,128)(2,1)S(1)} %queries.1), channel_id=1, source_target_pairs={{0,4},{4,0},{1,5},{5,1},{2,6},{6,2},{3,7},{7,3},{8,12},{12,8},{9,1... | collective-permute-start | bytes 98312 | tf_op jit(solution)/shard_map/ppermute | solution.py:327
  5.2 0.1 pad_add_fusion.ids_ref
  5.3 1.2 collective-permute-done
  6.6 4.0 %collective-permute-start.3 = (bf16[64,512]{1,0:T(8,128)(2,1)S(1)}, bf16[64,512]{1,0:T(8,128)(2,1)S(1)}, u32[]{:S(2)}, u32[]{:S(2)}) collective-permute-start(bf16[64,512]{1,0:T(8,128)(2,1)S(1)} %maximum_select_fusion.1.after_ref), channel_id=1, source_target_pairs={{0,24},{8,0},{16,8},{24,16},{1,25},{9,1},{17,9},{25,17},{2,26},{10... | collective-permute-start | bytes 196616 | tf_op jit(solution)/shard_map/ppermute | solution.py:327
  10.5 0.7 collective-permute-start.1
  11.3 3.4 %copy-done.9 = bf16[2048,2048]{1,0:T(8,128)(2,1)S(1)} copy-done((bf16[2048,2048]{1,0:T(8,128)(2,1)S(1)}, bf16[2048,2048]{1,0:T(8,128)(2,1)}, u32[]{:S(2)}) %copy-start.9) | copy-done | bytes 8388632
  14.6 5.2 %keys.1.k_ref = bf16[2048,512]{1,0:T(8,128)(2,1)S(1)} custom-call(bf16[2048,2048]{1,0:T(8,128)(2,1)S(1)} %copy-done.9, bf16[2048,512]{1,0:T(8,128)(2,1)S(1)} %copy-done.10, bf16[64,512]{1,0:T(8,128)(2,1)S(1)} %maximum_select_fusion.1.after_ref), custom_call_target="tpu_custom_call" | custom-call | flops 4294967296 | bytes 10485760 | tf_op jit(solution)/shard_map/keys/pallas_call | solution.py:80
  20.0 1.3 %collective-permute-start.8 = (bf16[256,512]{1,0:T(8,128)(2,1)S(1)}, bf16[256,512]{1,0:T(8,128)(2,1)S(1)}, u32[]{:S(2)}, u32[]{:S(2)}) collective-permute-start(bf16[256,512]{1,0:T(8,128)(2,1)S(1)} %pad_maximum_fusion.1.after_ref.q_ref), channel_id=1, source_target_pairs={{0,32},{32,64},{64,96},{96,0},{1,33},{33,65},{65,97},{97,1},{2,34}... | collective-permute-start | bytes 786440 | tf_op jit(solution)/shard_map/ppermute | solution.py:327
  21.3 2.4 %collective-permute-start.6 = (bf16[256,512]{1,0:T(8,128)(2,1)S(1)}, bf16[256,512]{1,0:T(8,128)(2,1)S(1)}, u32[]{:S(2)}, u32[]{:S(2)}) collective-permute-start(bf16[256,512]{1,0:T(8,128)(2,1)S(1)} %pad_maximum_fusion.1.after_ref.q_ref), channel_id=1, source_target_pairs={{0,64},{32,96},{64,0},{96,32},{1,65},{33,97},{65,1},{97,33},{2,66}... | collective-permute-start | bytes 786440 | tf_op jit(solution)/shard_map/ppermute | solution.py:327
  23.8 1.2 collective-permute-start.4
  24.9 5.1 %values.1.v_ref = bf16[2048,512]{1,0:T(8,128)(2,1)S(1)} custom-call(bf16[2048,2048]{1,0:T(8,128)(2,1)S(1)} %copy-done.9, bf16[2048,512]{1,0:T(8,128)(2,1)S(1)} %copy-done.11, bf16[256,512]{1,0:T(8,128)(2,1)S(1)} %pad_maximum_fusion.1.after_ref.q_ref), custom_call_target="tpu_custom_call" | custom-call | flops 4294967296 | bytes 10485760 | tf_op jit(solution)/shard_map/values/pallas_call | solution.py:80
  30.0 2.9 %collective-permute-done.4.q_ref = bf16[256,512]{1,0:T(8,128)(2,1)S(1)} collective-permute-done((bf16[256,512]{1,0:T(8,128)(2,1)S(1)}, bf16[256,512]{1,0:T(8,128)(2,1)S(1)}, u32[]{:S(2)}, u32[]{:S(2)}) %collective-permute-start.4) | collective-permute-done | bytes 262176 | tf_op jit(solution)/shard_map/ppermute | solution.py:327
  32.9 0.2 broadcast_in_dim.4.cut_ref
  33.1 3.5 %cross.5 = bf16[256,640]{1,0:T(8,128)(2,1)S(1)} custom-call(s32[3]{0:T(128)S(1)} %pad_add_fusion.ids_ref, s32[1024]{0:T(1024)S(1)} %copy-done.8, bf16[256,512]{1,0:T(8,128)(2,1)S(1)} %collective-permute-done.4.q_ref, bf16[2048,512]{1,0:T(8,128)(2,1)S(1)} %keys.1.k_ref, bf16[2048,512]{1,0:T(8,128)(2,1)S(1)} %values.1.v_ref, ...), custom_call_target="tpu_custom_call" | custom-call | flops 2147483648 | bytes 4194304 | tf_op jit(solution)/shard_map/cross/pallas_call | solution.py:172
  36.6 3.5 %collective-permute-start.5 = (bf16[256,640]{1,0:T(8,128)(2,1)S(1)}, bf16[256,640]{1,0:T(8,128)(2,1)S(1)}, u32[]{:S(2)}, u32[]{:S(2)}) collective-permute-start(bf16[256,640]{1,0:T(8,128)(2,1)S(1)} %cross.5), channel_id=1, source_target_pairs={{0,32},{32,64},{64,96},{96,0},{1,33},{33,65},{65,97},{97,1},{2,34}... | collective-permute-start | bytes 983048 | tf_op jit(solution)/shard_map/ppermute | solution.py:327
  40.2 3.7 %cross.6 = bf16[256,640]{1,0:T(8,128)(2,1)S(1)} custom-call(s32[3]{0:T(128)S(1)} %pad_add_fusion.ids_ref, s32[1024]{0:T(1024)S(1)} %copy-done.8, bf16[256,512]{1,0:T(8,128)(2,1)S(1)} %collective-permute-done.6.q_ref, bf16[2048,512]{1,0:T(8,128)(2,1)S(1)} %keys.1.k_ref, bf16[2048,512]{1,0:T(8,128)(2,1)S(1)} %values.1.v_ref, ...), custom_call_target="tpu_custom_call" | custom-call | flops 2147483648 | bytes 4194304 | tf_op jit(solution)/shard_map/cross/pallas_call | solution.py:172
  43.9 0.1 collective-permute-start.7
  44.0 3.5 %cross.7 = bf16[256,640]{1,0:T(8,128)(2,1)S(1)} custom-call(s32[3]{0:T(128)S(1)} %pad_add_fusion.ids_ref, s32[1024]{0:T(1024)S(1)} %copy-done.8, bf16[256,512]{1,0:T(8,128)(2,1)S(1)} %collective-permute-done.8.q_ref, bf16[2048,512]{1,0:T(8,128)(2,1)S(1)} %keys.1.k_ref, bf16[2048,512]{1,0:T(8,128)(2,1)S(1)} %values.1.v_ref, ...), custom_call_target="tpu_custom_call" | custom-call | flops 2147483648 | bytes 4194304 | tf_op jit(solution)/shard_map/cross/pallas_call | solution.py:172
  47.5 3.2 %collective-permute-start.9 = (bf16[256,640]{1,0:T(8,128)(2,1)S(1)}, bf16[256,640]{1,0:T(8,128)(2,1)S(1)}, u32[]{:S(2)}, u32[]{:S(2)}) collective-permute-start(bf16[256,640]{1,0:T(8,128)(2,1)S(1)} %cross.7), channel_id=1, source_target_pairs={{0,96},{32,0},{64,32},{96,64},{1,97},{33,1},{65,33},{97,65},{2,98}... | collective-permute-start | bytes 983048 | tf_op jit(solution)/shard_map/ppermute | solution.py:327
  50.7 4.0 %cross.4.a_ref = bf16[256,640]{1,0:T(8,128)(2,1)S(1)} custom-call(s32[3]{0:T(128)S(1)} %pad_add_fusion.ids_ref, s32[1024]{0:T(1024)S(1)} %copy-done.8, bf16[256,512]{1,0:T(8,128)(2,1)S(1)} %pad_maximum_fusion.1.after_ref.q_ref, bf16[2048,512]{1,0:T(8,128)(2,1)S(1)} %keys.1.k_ref, bf16[2048,512]{1,0:T(8,128)(2,1)S(1)} %values.1.v_ref, ...), custom_call_target="tpu_custom_call" | custom-call | flops 2147483648 | bytes 4194304 | tf_op jit(solution)/shard_map/cross/pallas_call | solution.py:172
  54.7 2.9 %collective-permute-done.9.d_ref = bf16[256,640]{1,0:T(8,128)(2,1)S(1)} collective-permute-done((bf16[256,640]{1,0:T(8,128)(2,1)S(1)}, bf16[256,640]{1,0:T(8,128)(2,1)S(1)}, u32[]{:S(2)}, u32[]{:S(2)}) %collective-permute-start.9) | collective-permute-done | bytes 327712 | tf_op jit(solution)/shard_map/ppermute | solution.py:327
  57.6 1.0 blend.1
  58.6 11.2 %all_to_all.10.parts_ref = bf16[8,32,640]{2,1,0:T(8,128)(2,1)S(1)} all-to-all(bf16[8,32,640]{2,1,0:T(8,128)(2,1)S(1)} %bitcast.17), channel_id=1, replica_groups=mesh['x'=4,'z'=4,'y_lo'=2,'y_hi'=2,'core'=2] {'z','y_lo'}, dimensions={0} | all-to-all | bytes 655360 | tf_op jit(solution)/shard_map/all_to_all | solution.py:379
  69.8 0.7 cross_output.1
  70.5 3.6 %collective-permute-start.10 = (bf16[32,2048]{1,0:T(8,128)(2,1)S(1)}, bf16[32,2048]{1,0:T(8,128)(2,1)S(1)}, u32[]{:S(2)}, u32[]{:S(2)}) collective-permute-start(bf16[32,2048]{1,0:T(8,128)(2,1)S(1)} %cross_output.1), channel_id=1, source_target_pairs={{0,1},{1,0},{2,3},{3,2},{4,5},{5,4},{6,7},{7,6},{8,9},{9,8},{10,11... | collective-permute-start | bytes 393224 | tf_op jit(solution)/shard_map/ppermute | solution.py:327
  74.1 1.0 collective-permute-done.10
  75.1 2.7 %collective-permute-start.11 = (bf16[32,2048]{1,0:T(8,128)(2,1)S(1)}, bf16[32,2048]{1,0:T(8,128)(2,1)S(1)}, u32[]{:S(2)}, u32[]{:S(2)}) collective-permute-start(bf16[32,2048]{1,0:T(8,128)(2,1)S(1)} %add_convert_fusion.2.one_ref), channel_id=1, source_target_pairs={{0,2},{2,0},{1,3},{3,1},{4,6},{6,4},{5,7},{7,5},{8,10},{10,8},{9,1... | collective-permute-start | bytes 393224 | tf_op jit(solution)/shard_map/ppermute | solution.py:327
  77.9 3.6 %collective-permute-done.11.two_ref = bf16[32,2048]{1,0:T(8,128)(2,1)S(1)} collective-permute-done((bf16[32,2048]{1,0:T(8,128)(2,1)S(1)}, bf16[32,2048]{1,0:T(8,128)(2,1)S(1)}, u32[]{:S(2)}, u32[]{:S(2)}) %collective-permute-start.11) | collective-permute-done | bytes 131104 | tf_op jit(solution)/shard_map/ppermute | solution.py:327
  81.5 1.8 %self_project.1 = (f32[32,2048]{1,0:T(8,128)S(1)}, bf16[32,384]{1,0:T(8,128)(2,1)S(1)}, bf16[32,384]{1,0:T(8,128)(2,1)S(1)}, bf16[32,384]{1,0:T(8,128)(2,1)S(1)}, bf16[32,384]{1,0:T(8,128)(2,1)S(1)}) custom-call(s32[3]{0:T(128)S(1)} %pad_add_fusion.ids_ref, bf16[32,2048]{1,0:T(8,128)(2,1)S(1)} %copy-done.7, bf16[32,2048]{1,0:T(8,128)(2,1)S(1)} %add_convert_fusion.2.one_ref, ...), custom_call_target="tpu_custom_call" | custom-call | tf_op jit(solution)/shard_map/self_project/pallas_call | solution.py:258
  83.3 3.6 %collective-permute-start.12 = (bf16[32,384]{1,0:T(8,128)(2,1)S(1)}, bf16[32,384]{1,0:T(8,128)(2,1)S(1)}, u32[]{:S(2)}, u32[]{:S(2)}) collective-permute-start(bf16[32,384]{1,0:T(8,128)(2,1)S(1)} %get-tuple-element.16), channel_id=1, source_target_pairs={{0,32},{32,64},{64,96},{96,0},{1,33},{33,65},{65,97},{97,1},{2,34}... | collective-permute-start | bytes 73736 | tf_op jit(solution)/shard_map/ppermute | solution.py:327
  86.9 0.2 collective-permute-start.13
  87.1 2.3 %collective-permute-start.14 = (bf16[32,384]{1,0:T(8,128)(2,1)S(1)}, bf16[32,384]{1,0:T(8,128)(2,1)S(1)}, u32[]{:S(2)}, u32[]{:S(2)}) collective-permute-start(bf16[32,384]{1,0:T(8,128)(2,1)S(1)} %get-tuple-element.18), channel_id=1, source_target_pairs={{0,96},{32,0},{64,32},{96,64},{1,97},{33,1},{65,33},{97,65},{2,98}... | collective-permute-start | bytes 73736 | tf_op jit(solution)/shard_map/ppermute | solution.py:327
  89.4 1.7 %collective-permute-done.13.c_ref = bf16[32,384]{1,0:T(8,128)(2,1)S(1)} collective-permute-done((bf16[32,384]{1,0:T(8,128)(2,1)S(1)}, bf16[32,384]{1,0:T(8,128)(2,1)S(1)}, u32[]{:S(2)}, u32[]{:S(2)}) %collective-permute-start.13) | collective-permute-done | bytes 24608 | tf_op jit(solution)/shard_map/ppermute | solution.py:327
  91.1 10.0 %all_to_all.11.kv_ref = bf16[8,128,256]{2,1,0:T(8,128)(2,1)S(1)} all-to-all(bf16[8,128,256]{2,1,0:T(8,128)(2,1)S(1)} %broadcast_in_dim.5), channel_id=1, replica_groups=mesh['x'=4,'z'=4,'y_lo'=2,'y_hi'=2,'core'=2] {'z','y_lo'}, dimensions={0} | all-to-all | bytes 1048576 | tf_op jit(solution)/shard_map/all_to_all | solution.py:386
  101.1 1.1 self_attend.1
  102.3 2.2 %collective-permute-start.15 = (bf16[32,128]{1,0:T(8,128)(2,1)S(1)}, bf16[32,128]{1,0:T(8,128)(2,1)S(1)}, u32[]{:S(2)}, u32[]{:S(2)}) collective-permute-start(bf16[32,128]{1,0:T(8,128)(2,1)S(1)} %get-tuple-element.20), channel_id=1, source_target_pairs={{0,96},{32,0},{64,32},{96,64},{1,97},{33,1},{65,33},{97,65},{2,98}... | collective-permute-start | bytes 24584 | tf_op jit(solution)/shard_map/ppermute | solution.py:327
  104.5 0.7 collective-permute-start.17
  105.2 0.1 collective-permute-done.15.b_ref
  105.3 3.2 %collective-permute-done.16.c_ref = bf16[32,128]{1,0:T(8,128)(2,1)S(1)} collective-permute-done((bf16[32,128]{1,0:T(8,128)(2,1)S(1)}, bf16[32,128]{1,0:T(8,128)(2,1)S(1)}, u32[]{:S(2)}, u32[]{:S(2)}) %collective-permute-start.16) | collective-permute-done | bytes 8224 | tf_op jit(solution)/shard_map/ppermute | solution.py:327
  108.5 1.0 self_output.1
  109.5 5.2 %collective-permute-start.18 = (bf16[32,2048]{1,0:T(8,128)(2,1)S(1)}, bf16[32,2048]{1,0:T(8,128)(2,1)S(1)}, u32[]{:S(2)}, u32[]{:S(2)}) collective-permute-start(bf16[32,2048]{1,0:T(8,128)(2,1)S(1)} %self_output.1), channel_id=1, source_target_pairs={{0,1},{1,0},{2,3},{3,2},{4,5},{5,4},{6,7},{7,6},{8,9},{9,8},{10,11... | collective-permute-start | bytes 393224 | tf_op jit(solution)/shard_map/ppermute | solution.py:327
  114.7 1.0 collective-permute-done.18
  115.7 2.7 %collective-permute-start.19 = (bf16[32,2048]{1,0:T(8,128)(2,1)S(1)}, bf16[32,2048]{1,0:T(8,128)(2,1)S(1)}, u32[]{:S(2)}, u32[]{:S(2)}) collective-permute-start(bf16[32,2048]{1,0:T(8,128)(2,1)S(1)} %add_convert_fusion.1), channel_id=1, source_target_pairs={{0,2},{2,0},{1,3},{3,1},{4,6},{6,4},{5,7},{7,5},{8,10},{10,8},{9,1... | collective-permute-start | bytes 393224 | tf_op jit(solution)/shard_map/ppermute | solution.py:327
  118.5 3.6 %collective-permute-done.19 = bf16[32,2048]{1,0:T(8,128)(2,1)S(1)} collective-permute-done((bf16[32,2048]{1,0:T(8,128)(2,1)S(1)}, bf16[32,2048]{1,0:T(8,128)(2,1)S(1)}, u32[]{:S(2)}, u32[]{:S(2)}) %collective-permute-start.19) | collective-permute-done | bytes 131104 | tf_op jit(solution)/shard_map/ppermute | solution.py:327
  122.0 0.7 add_convert_fusion
  (46 shorter events, 0.3 us)
Async XLA Ops:
  0.0 1.6 %copy-start.2 = (bf16[2048,512]{1,0:T(8,128)(2,1)S(1)}, bf16[2048,512]{1,0:T(8,128)(2,1)}, u32[]{:S(2)}) copy-start(bf16[2048,512]{1,0:T(8,128)(2,1)} %wq_ref.2) | copy-start | bytes 6291460
  1.6 0.9 copy-start.6
  2.5 8.8 %copy-start.10 = (bf16[2048,512]{1,0:T(8,128)(2,1)S(1)}, bf16[2048,512]{1,0:T(8,128)(2,1)}, u32[]{:S(2)}) copy-start(bf16[2048,512]{1,0:T(8,128)(2,1)} %w_ref.2) | copy-start | bytes 6291460
  3.0 3.5 %collective-permute-start = (bf16[32,512]{1,0:T(8,128)(2,1)S(1)}, bf16[32,512]{1,0:T(8,128)(2,1)S(1)}, u32[]{:S(2)}, u32[]{:S(2)}) collective-permute-start(bf16[32,512]{1,0:T(8,128)(2,1)S(1)} %queries.1), channel_id=1, source_target_pairs={{0,4},{4,0},{1,5},{5,1},{2,6},{6,2},{3,7},{7,3},{8,12},{12,8},{9,1... | collective-permute-start | bytes 98312 | tf_op jit(solution)/shard_map/ppermute | solution.py:327
  6.6 13.3 %collective-permute-start.3 = (bf16[64,512]{1,0:T(8,128)(2,1)S(1)}, bf16[64,512]{1,0:T(8,128)(2,1)S(1)}, u32[]{:S(2)}, u32[]{:S(2)}) collective-permute-start(bf16[64,512]{1,0:T(8,128)(2,1)S(1)} %maximum_select_fusion.1.after_ref), channel_id=1, source_target_pairs={{0,24},{8,0},{16,8},{24,16},{1,25},{9,1},{17,9},{25,17},{2,26},{10... | collective-permute-start | bytes 196616 | tf_op jit(solution)/shard_map/ppermute | solution.py:327
  10.5 9.3 %collective-permute-start.2 = (bf16[64,512]{1,0:T(8,128)(2,1)S(1)}, bf16[64,512]{1,0:T(8,128)(2,1)S(1)}, u32[]{:S(2)}, u32[]{:S(2)}) collective-permute-start(bf16[64,512]{1,0:T(8,128)(2,1)S(1)} %maximum_select_fusion.1.after_ref), channel_id=1, source_target_pairs={{0,16},{8,24},{16,0},{24,8},{1,17},{9,25},{17,1},{25,9},{2,18},{10... | collective-permute-start | bytes 196616 | tf_op jit(solution)/shard_map/ppermute | solution.py:327
  10.5 9.3 %collective-permute-start.1 = (bf16[64,512]{1,0:T(8,128)(2,1)S(1)}, bf16[64,512]{1,0:T(8,128)(2,1)S(1)}, u32[]{:S(2)}, u32[]{:S(2)}) collective-permute-start(bf16[64,512]{1,0:T(8,128)(2,1)S(1)} %maximum_select_fusion.1.after_ref), channel_id=1, source_target_pairs={{0,8},{8,16},{16,24},{24,0},{1,9},{9,17},{17,25},{25,1},{2,10},{10... | collective-permute-start | bytes 196616 | tf_op jit(solution)/shard_map/ppermute | solution.py:327
  11.3 3.4 %copy-start.9 = (bf16[2048,2048]{1,0:T(8,128)(2,1)S(1)}, bf16[2048,2048]{1,0:T(8,128)(2,1)}, u32[]{:S(2)}) copy-start(bf16[2048,2048]{1,0:T(8,128)(2,1)} %context_ref.3) | copy-start | bytes 25165828
  14.6 10.3 %copy-start.11 = (bf16[2048,512]{1,0:T(8,128)(2,1)S(1)}, bf16[2048,512]{1,0:T(8,128)(2,1)}, u32[]{:S(2)}) copy-start(bf16[2048,512]{1,0:T(8,128)(2,1)} %w_ref.3) | copy-start | bytes 6291460
  20.0 12.9 %copy-start.8 = (s32[1024]{0:T(1024)S(1)}, s32[1024]{0:T(1024)}, u32[]{:S(2)}) copy-start(s32[1024]{0:T(1024)} %cutoff_ref.7) | copy-start | bytes 12292
  20.0 23.9 %collective-permute-start.8 = (bf16[256,512]{1,0:T(8,128)(2,1)S(1)}, bf16[256,512]{1,0:T(8,128)(2,1)S(1)}, u32[]{:S(2)}, u32[]{:S(2)}) collective-permute-start(bf16[256,512]{1,0:T(8,128)(2,1)S(1)} %pad_maximum_fusion.1.after_ref.q_ref), channel_id=1, source_target_pairs={{0,32},{32,64},{64,96},{96,0},{1,33},{33,65},{65,97},{97,1},{2,34}... | collective-permute-start | bytes 786440 | tf_op jit(solution)/shard_map/ppermute | solution.py:327
  21.3 18.8 %collective-permute-start.6 = (bf16[256,512]{1,0:T(8,128)(2,1)S(1)}, bf16[256,512]{1,0:T(8,128)(2,1)S(1)}, u32[]{:S(2)}, u32[]{:S(2)}) collective-permute-start(bf16[256,512]{1,0:T(8,128)(2,1)S(1)} %pad_maximum_fusion.1.after_ref.q_ref), channel_id=1, source_target_pairs={{0,64},{32,96},{64,0},{96,32},{1,65},{33,97},{65,1},{97,33},{2,66}... | collective-permute-start | bytes 786440 | tf_op jit(solution)/shard_map/ppermute | solution.py:327
  23.8 9.2 %collective-permute-start.4 = (bf16[256,512]{1,0:T(8,128)(2,1)S(1)}, bf16[256,512]{1,0:T(8,128)(2,1)S(1)}, u32[]{:S(2)}, u32[]{:S(2)}) collective-permute-start(bf16[256,512]{1,0:T(8,128)(2,1)S(1)} %pad_maximum_fusion.1.after_ref.q_ref), channel_id=1, source_target_pairs={{0,96},{32,0},{64,32},{96,64},{1,97},{33,1},{65,33},{97,65},{2,98}... | collective-permute-start | bytes 786440 | tf_op jit(solution)/shard_map/ppermute | solution.py:327
  36.6 18.0 %collective-permute-start.5 = (bf16[256,640]{1,0:T(8,128)(2,1)S(1)}, bf16[256,640]{1,0:T(8,128)(2,1)S(1)}, u32[]{:S(2)}, u32[]{:S(2)}) collective-permute-start(bf16[256,640]{1,0:T(8,128)(2,1)S(1)} %cross.5), channel_id=1, source_target_pairs={{0,32},{32,64},{64,96},{96,0},{1,33},{33,65},{65,97},{97,1},{2,34}... | collective-permute-start | bytes 983048 | tf_op jit(solution)/shard_map/ppermute | solution.py:327
  43.9 10.8 %collective-permute-start.7 = (bf16[256,640]{1,0:T(8,128)(2,1)S(1)}, bf16[256,640]{1,0:T(8,128)(2,1)S(1)}, u32[]{:S(2)}, u32[]{:S(2)}) collective-permute-start(bf16[256,640]{1,0:T(8,128)(2,1)S(1)} %cross.6), channel_id=1, source_target_pairs={{0,64},{32,96},{64,0},{96,32},{1,65},{33,97},{65,1},{97,33},{2,66}... | collective-permute-start | bytes 983048 | tf_op jit(solution)/shard_map/ppermute | solution.py:327
  47.5 10.1 %collective-permute-start.9 = (bf16[256,640]{1,0:T(8,128)(2,1)S(1)}, bf16[256,640]{1,0:T(8,128)(2,1)S(1)}, u32[]{:S(2)}, u32[]{:S(2)}) collective-permute-start(bf16[256,640]{1,0:T(8,128)(2,1)S(1)} %cross.7), channel_id=1, source_target_pairs={{0,96},{32,0},{64,32},{96,64},{1,97},{33,1},{65,33},{97,65},{2,98}... | collective-permute-start | bytes 983048 | tf_op jit(solution)/shard_map/ppermute | solution.py:327
  50.7 30.8 %copy-start.4 = (bf16[2048,512]{1,0:T(8,128)(2,1)S(1)}, bf16[2048,512]{1,0:T(8,128)(2,1)}, u32[]{:S(2)}) copy-start(bf16[2048,512]{1,0:T(8,128)(2,1)} %wk_ref.1) | copy-start | bytes 6291460
  50.7 30.8 %copy-start.5 = (bf16[2048,512]{1,0:T(8,128)(2,1)S(1)}, bf16[2048,512]{1,0:T(8,128)(2,1)}, u32[]{:S(2)}) copy-start(bf16[2048,512]{1,0:T(8,128)(2,1)} %wv_ref.1) | copy-start | bytes 6291460
  54.6 15.1 %copy-start = (bf16[512,2048]{1,0:T(8,128)(2,1)S(1)}, bf16[512,2048]{1,0:T(8,128)(2,1)}, u32[]{:S(2)}) copy-start(bf16[512,2048]{1,0:T(8,128)(2,1)} %wo_ref.2) | copy-start | bytes 6291460
  58.6 22.9 %copy-start.3 = (bf16[2048,512]{1,0:T(8,128)(2,1)S(1)}, bf16[2048,512]{1,0:T(8,128)(2,1)}, u32[]{:S(2)}) copy-start(bf16[2048,512]{1,0:T(8,128)(2,1)} %wq_ref.3) | copy-start | bytes 6291460
  58.6 22.9 %copy-start.7 = (bf16[32,2048]{1,0:T(8,128)(2,1)S(1)}, bf16[32,2048]{1,0:T(8,128)(2,1)}, u32[]{:S(2)}) copy-start(bf16[32,2048]{1,0:T(8,128)(2,1)} %latent_ref.3) | copy-start | bytes 393220
  70.5 4.6 %collective-permute-start.10 = (bf16[32,2048]{1,0:T(8,128)(2,1)S(1)}, bf16[32,2048]{1,0:T(8,128)(2,1)S(1)}, u32[]{:S(2)}, u32[]{:S(2)}) collective-permute-start(bf16[32,2048]{1,0:T(8,128)(2,1)S(1)} %cross_output.1), channel_id=1, source_target_pairs={{0,1},{1,0},{2,3},{3,2},{4,5},{5,4},{6,7},{7,6},{8,9},{9,8},{10,11... | collective-permute-start | bytes 393224 | tf_op jit(solution)/shard_map/ppermute | solution.py:327
  75.1 6.3 %collective-permute-start.11 = (bf16[32,2048]{1,0:T(8,128)(2,1)S(1)}, bf16[32,2048]{1,0:T(8,128)(2,1)S(1)}, u32[]{:S(2)}, u32[]{:S(2)}) collective-permute-start(bf16[32,2048]{1,0:T(8,128)(2,1)S(1)} %add_convert_fusion.2.one_ref), channel_id=1, source_target_pairs={{0,2},{2,0},{1,3},{3,1},{4,6},{6,4},{5,7},{7,5},{8,10},{10,8},{9,1... | collective-permute-start | bytes 393224 | tf_op jit(solution)/shard_map/ppermute | solution.py:327
  83.3 25.2 %copy-start.1 = (bf16[512,2048]{1,0:T(8,128)(2,1)S(1)}, bf16[512,2048]{1,0:T(8,128)(2,1)}, u32[]{:S(2)}) copy-start(bf16[512,2048]{1,0:T(8,128)(2,1)} %wo_ref.3) | copy-start | bytes 6291460
  83.3 6.0 %collective-permute-start.12 = (bf16[32,384]{1,0:T(8,128)(2,1)S(1)}, bf16[32,384]{1,0:T(8,128)(2,1)S(1)}, u32[]{:S(2)}, u32[]{:S(2)}) collective-permute-start(bf16[32,384]{1,0:T(8,128)(2,1)S(1)} %get-tuple-element.16), channel_id=1, source_target_pairs={{0,32},{32,64},{64,96},{96,0},{1,33},{33,65},{65,97},{97,1},{2,34}... | collective-permute-start | bytes 73736 | tf_op jit(solution)/shard_map/ppermute | solution.py:327
  86.9 4.2 %collective-permute-start.13 = (bf16[32,384]{1,0:T(8,128)(2,1)S(1)}, bf16[32,384]{1,0:T(8,128)(2,1)S(1)}, u32[]{:S(2)}, u32[]{:S(2)}) collective-permute-start(bf16[32,384]{1,0:T(8,128)(2,1)S(1)} %get-tuple-element.17), channel_id=1, source_target_pairs={{0,64},{32,96},{64,0},{96,32},{1,65},{33,97},{65,1},{97,33},{2,66}... | collective-permute-start | bytes 73736 | tf_op jit(solution)/shard_map/ppermute | solution.py:327
  87.1 4.0 %collective-permute-start.14 = (bf16[32,384]{1,0:T(8,128)(2,1)S(1)}, bf16[32,384]{1,0:T(8,128)(2,1)S(1)}, u32[]{:S(2)}, u32[]{:S(2)}) collective-permute-start(bf16[32,384]{1,0:T(8,128)(2,1)S(1)} %get-tuple-element.18), channel_id=1, source_target_pairs={{0,96},{32,0},{64,32},{96,64},{1,97},{33,1},{65,33},{97,65},{2,98}... | collective-permute-start | bytes 73736 | tf_op jit(solution)/shard_map/ppermute | solution.py:327
  102.3 3.0 %collective-permute-start.15 = (bf16[32,128]{1,0:T(8,128)(2,1)S(1)}, bf16[32,128]{1,0:T(8,128)(2,1)S(1)}, u32[]{:S(2)}, u32[]{:S(2)}) collective-permute-start(bf16[32,128]{1,0:T(8,128)(2,1)S(1)} %get-tuple-element.20), channel_id=1, source_target_pairs={{0,96},{32,0},{64,32},{96,64},{1,97},{33,1},{65,33},{97,65},{2,98}... | collective-permute-start | bytes 24584 | tf_op jit(solution)/shard_map/ppermute | solution.py:327
  104.5 4.0 %collective-permute-start.16 = (bf16[32,128]{1,0:T(8,128)(2,1)S(1)}, bf16[32,128]{1,0:T(8,128)(2,1)S(1)}, u32[]{:S(2)}, u32[]{:S(2)}) collective-permute-start(bf16[32,128]{1,0:T(8,128)(2,1)S(1)} %get-tuple-element.21), channel_id=1, source_target_pairs={{0,64},{32,96},{64,0},{96,32},{1,65},{33,97},{65,1},{97,33},{2,66}... | collective-permute-start | bytes 24584 | tf_op jit(solution)/shard_map/ppermute | solution.py:327
  104.5 4.0 %collective-permute-start.17 = (bf16[32,128]{1,0:T(8,128)(2,1)S(1)}, bf16[32,128]{1,0:T(8,128)(2,1)S(1)}, u32[]{:S(2)}, u32[]{:S(2)}) collective-permute-start(bf16[32,128]{1,0:T(8,128)(2,1)S(1)} %get-tuple-element.22), channel_id=1, source_target_pairs={{0,32},{32,64},{64,96},{96,0},{1,33},{33,65},{65,97},{97,1},{2,34}... | collective-permute-start | bytes 24584 | tf_op jit(solution)/shard_map/ppermute | solution.py:327
  109.5 6.2 %collective-permute-start.18 = (bf16[32,2048]{1,0:T(8,128)(2,1)S(1)}, bf16[32,2048]{1,0:T(8,128)(2,1)S(1)}, u32[]{:S(2)}, u32[]{:S(2)}) collective-permute-start(bf16[32,2048]{1,0:T(8,128)(2,1)S(1)} %self_output.1), channel_id=1, source_target_pairs={{0,1},{1,0},{2,3},{3,2},{4,5},{5,4},{6,7},{7,6},{8,9},{9,8},{10,11... | collective-permute-start | bytes 393224 | tf_op jit(solution)/shard_map/ppermute | solution.py:327
  115.7 6.3 %collective-permute-start.19 = (bf16[32,2048]{1,0:T(8,128)(2,1)S(1)}, bf16[32,2048]{1,0:T(8,128)(2,1)S(1)}, u32[]{:S(2)}, u32[]{:S(2)}) collective-permute-start(bf16[32,2048]{1,0:T(8,128)(2,1)S(1)} %add_convert_fusion.1), channel_id=1, source_target_pairs={{0,2},{2,0},{1,3},{3,1},{4,6},{6,4},{5,7},{7,5},{8,10},{10,8},{9,1... | collective-permute-start | bytes 393224 | tf_op jit(solution)/shard_map/ppermute | solution.py:327
where the time goes:
time: 123 us
  starting transfers between devices  41.7 us (34%)
  Pallas kernels  31.2 us (25%)
  waiting for transfers between devices  21.2 us (17%)
  blocking collectives  21.2 us (17%)
  local copies, waits for them, and re-layouts  6.18 us (5%)
    ppermute x20, starting transfers between devices, moved(): lax.ppermute(tensor, axis, [(i, (i + offset) % size) for i in range(size)])  41.7 us
    ppermute x20, waiting for transfers between devices, moved(): lax.ppermute(tensor, axis, [(i, (i + offset) % size) for i in range(size)])  21.2 us
    pallas_call x4, Pallas kernels, cross_attend(): pl.pallas_call(functools.partial(cross_kernel, offset), out_shape=shape_o...  14.7 us
    all_to_all x1, blocking collectives, on_device(): mixed = lax.all_to_all(mixed, ('z', 'y_lo'), 0, 0)  11.2 us
    pallas_call x2, Pallas kernels, project_context(): pl.pallas_call(functools.partial(context_kernel, min(512, rows)), out_sha...  10.3 us
    all_to_all x1, blocking collectives, on_device(): lax.all_to_all(jnp.broadcast_to(kv[None], (8,) + kv.shape), ('z', 'y_lo')...  9.99 us
    unnamed x24, local copies, waits for them, and re-layouts  5.92 us
  transfers between devices with their start and end apart: 20, of which 10 were waited for; matrix products, arithmetic and copies ran while one was open for 0% of the time, Pallas kernels for 20%

commit v1 on v0

--- a/solution.py
+++ b/solution.py
@@ -2,6 +2,7 @@
 
 import jax
 import jax.numpy as jnp
+import numpy as np
 from jax import lax
 from jax.experimental import pallas as pl
 from jax.experimental.pallas import tpu as pltpu
@@ -269,7 +270,7 @@
 def self_kernel(ids_ref, a_ref, b_ref, c_ref, d_ref, kv_ref, *outs):
     rows = a_ref.shape[0]
     groups, group_rows, _ = kv_ref.shape
-    own_x, own_zy = ids_ref[0], ids_ref[1]
+    own_a, own_b, stride_a, stride_b, own_y = (ids_ref[i] for i in (0, 1, 3, 4, 5))
     q = jnp.concatenate([ref[:, :HEAD_DIM] for ref in (a_ref, b_ref, c_ref, d_ref)], axis=0)
     k = jnp.concatenate([kv_ref[i, :, :HEAD_DIM] for i in range(groups)], axis=0)
     v = jnp.concatenate([kv_ref[i, :, HEAD_DIM:] for i in range(groups)], axis=0)
@@ -277,11 +278,11 @@
     q_row = lax.broadcasted_iota(jnp.int32, scores.shape, 0)
     k_row = lax.broadcasted_iota(jnp.int32, scores.shape, 1)
     shift = rows.bit_length() - 1
-    q_x = (own_x - (q_row >> shift)) & 3
-    q_place = (q_x * groups + own_zy) * rows + (q_row & (rows - 1))
+    q_a = (own_a - (q_row >> shift)) & 3
+    q_place = q_a * stride_a + (q_row & (rows - 1)) + (own_b * stride_b + own_y * rows)
     group = k_row >> (group_rows.bit_length() - 1)
-    k_x = (own_x - (k_row >> shift)) & 3
-    k_place = (k_x * groups + group) * rows + (k_row & (rows - 1))
+    k_a = (own_a - (k_row >> shift)) & 3
+    k_place = k_a * stride_a + (group >> 1) * stride_b + (group & 1) * rows + (k_row & (rows - 1))
     scores = jnp.where(k_place <= q_place, scores, MASKED_SCORE)
     peak = jnp.max(scores, axis=1, keepdims=True)
     probs = jnp.exp2(scores - peak).astype(BF16)
@@ -325,6 +326,33 @@
 
 def moved(tensor, axis, size, offset):
     return lax.ppermute(tensor, axis, [(i, (i + offset) % size) for i in range(size)])
+
+
+PLANE = ("x", "z", "core")
+WHOLE = ("x", "z", "y_lo", "y_hi", "core")
+
+
+def turned(tensor, axis, offset):
+    pairs = []
+    for x in range(4):
+        for z in range(4):
+            for core in range(2):
+                if (axis == "a") == (core == 0):
+                    to = ((x + offset) % 4, z)
+                else:
+                    to = (x, (z + offset) % 4)
+                pairs.append(((x * 4 + z) * 2 + core, (to[0] * 4 + to[1]) * 2 + core))
+    return lax.ppermute(tensor, PLANE, pairs)
+
+
+def exchanged(tensor):
+    order = np.arange(128).reshape(4, 4, 2, 2, 2)
+    groups = []
+    for y_hi in range(2):
+        for a in range(4):
+            groups.append(order[a, :, :, y_hi, 0].reshape(-1).tolist())
+            groups.append(order[:, a, :, y_hi, 1].reshape(-1).tolist())
+    return lax.all_to_all(tensor, WHOLE, 0, 0, axis_index_groups=groups)
 
 
 def summed_over_tp(part):
@@ -346,46 +374,51 @@
     wv_self,
     wo_self,
 ):
-    x = lax.axis_index("x")
-    zy = lax.axis_index("z") * 2 + lax.axis_index("y_lo")
-    ids = jnp.stack([x, zy, (x * 8 + zy) * context.shape[0]]).astype(jnp.int32)
+    x, z, y_lo = lax.axis_index("x"), lax.axis_index("z"), lax.axis_index("y_lo")
+    first_core = lax.axis_index("core") == 0
+    a = jnp.where(first_core, x, z)
+    b = jnp.where(first_core, z, x)
+    rows = latent_in.shape[0]
+    stride_a = jnp.where(first_core, 8 * rows, 2 * rows)
+    stride_b = jnp.where(first_core, 2 * rows, 8 * rows)
+    first_pos = ((x * 4 + z) * 2 + y_lo) * context.shape[0]
+    ids = jnp.stack([a, b, first_pos, stride_a, stride_b, y_lo]).astype(jnp.int32)
+    turned_cutoff = cutoff.reshape(4, 4, 2 * rows).transpose(1, 0, 2).reshape(-1)
+    cutoff = jnp.where(first_core, cutoff, turned_cutoff)
     cut_wide = jnp.broadcast_to(cutoff[:, None], (cutoff.shape[0], HEAD_DIM))
 
     own = project_queries(latent_in, wq_cross)
     other = moved(own, "y_lo", 2, 1)
-    y_lo = lax.axis_index("y_lo")
     pair = jnp.where(
         y_lo == 0, jnp.concatenate([own, other]), jnp.concatenate([other, own])
     )
     keys = project_context(context, wk_cross, pair, "keys")
-    z = lax.axis_index("z")
-    ring = [pair] + [moved(pair, "z", 4, offset) for offset in (1, 2, 3)]
+    ring = [pair] + [turned(pair, "b", offset) for offset in (1, 2, 3)]
     pieces = [
-        lax.dynamic_index_in_dim(jnp.stack(ring), (z - place) % 4, 0, False) for place in range(4)
+        lax.dynamic_index_in_dim(jnp.stack(ring), (b - place) & 3, 0, False) for place in range(4)
     ]
     mine = jnp.concatenate(pieces)
     values = project_context(context, wv_cross, mine, "values")
     blocks = {0: mine}
     for offset in (2, 3, 1):
-        blocks[(4 - offset) % 4] = moved(mine, "x", 4, offset)
+        blocks[(4 - offset) % 4] = turned(mine, "a", offset)
 
     parts = []
-    for offset in (0, 1, 2, 3):
+    for offset in (2, 1, 3, 0):
         part = cross_attend(offset, ids, cutoff, blocks[offset], keys, values, cut_wide)
-        parts.append(moved(part, "x", 4, offset) if offset else part)
+        parts.append(turned(part, "a", offset) if offset else part)
     mixed = blend_parts(parts)
-    rows = latent_in.shape[0]
     mixed = mixed.reshape(8, rows, mixed.shape[1])
-    mixed = lax.all_to_all(mixed, ("z", "y_lo"), 0, 0)
+    mixed = exchanged(mixed)
     cross_part = cross_output(mixed, wo_cross)
     one, two = summed_over_tp(cross_part)
 
     state, *sent = self_project(ids, latent_in, one, two, wq_self, wk_self, wv_self)
-    parts = [sent[0]] + [moved(sent[o], "x", 4, o) for o in (1, 2, 3)]
+    parts = [sent[0]] + [turned(sent[o], "a", o) for o in (1, 2, 3)]
     kv = jnp.concatenate([part[:, HEAD_DIM:] for part in parts])
-    kv = lax.all_to_all(jnp.broadcast_to(kv[None], (8,) + kv.shape), ("z", "y_lo"), 0, 0)
+    kv = exchanged(jnp.broadcast_to(kv[None], (8,) + kv.shape))
     outs = self_attend(ids, parts, kv)
-    outs = [outs[0]] + [moved(outs[o], "x", 4, -o) for o in (1, 2, 3)]
+    outs = [outs[0]] + [turned(outs[o], "a", -o) for o in (1, 2, 3)]
     self_part = self_output(ids, outs, wo_self)
     one, two = summed_over_tp(self_part)
     return (state + (one.astype(F32) + two.astype(F32))).astype(BF16)

time: 123 us -> 115 us (0.935)
  waiting for transfers between devices: 21.2 us -> 17.2 us
  starting transfers between devices: 41.7 us -> 38.8 us
    ppermute x20 -> x5, starting transfers between devices: 41.7 us -> 18.5 us  [moved(): lax.ppermute(tensor, axis, [(i, (i + offset) % size) for i in range(size)])]
    ppermute x0 -> x15, starting transfers between devices: none -> 20.3 us  [turned(): return lax.ppermute(tensor, PLANE, pairs)]
    ppermute x20 -> x5, waiting for transfers between devices: 21.2 us -> 10.2 us  [moved(): lax.ppermute(tensor, axis, [(i, (i + offset) % size) for i in range(size)])]
    ppermute x0 -> x15, waiting for transfers between devices: none -> 6.98 us  [turned(): return lax.ppermute(tensor, PLANE, pairs)]
  transfers between devices with their start and end apart: 20 -> 20, of which waited for: 10 -> 13; matrix products, arithmetic and copies ran while one was open for 0% -> 0% of each run, Pallas kernels for 20% -> 21%
where the time goes in v1:
time: 115 us; the launch traced here: 114 us
  starting transfers between devices  38.8 us (34%)
  Pallas kernels  30.3 us (26%)
  blocking collectives  20.6 us (18%)
  waiting for transfers between devices  17.2 us (15%)
  local copies, waits for them, and re-layouts  6.43 us (6%)
    all_to_all x2, blocking collectives, exchanged(): return lax.all_to_all(tensor, WHOLE, 0, 0, axis_index_groups=groups)  20.6 us
    ppermute x15, starting transfers between devices, turned(): return lax.ppermute(tensor, PLANE, pairs)  20.3 us
    ppermute x5, starting transfers between devices, moved(): lax.ppermute(tensor, axis, [(i, (i + offset) % size) for i in range(size)])  18.5 us
    pallas_call x4, Pallas kernels, cross_attend(): pl.pallas_call(functools.partial(cross_kernel, offset), out_shape=shape_o...  13.9 us
    ppermute x5, waiting for transfers between devices, moved(): lax.ppermute(tensor, axis, [(i, (i + offset) % size) for i in range(size)])  10.2 us
    pallas_call x2, Pallas kernels, project_context(): pl.pallas_call(functools.partial(context_kernel, min(512, rows)), out_sha...  10.1 us
    ppermute x15, waiting for transfers between devices, turned(): return lax.ppermute(tensor, PLANE, pairs)  6.98 us
    unnamed x24, local copies, waits for them, and re-layouts  5.92 us
  transfers between devices with their start and end apart: 20, of which 13 were waited for; matrix products, arithmetic and copies ran while one was open for 0% of the time, Pallas kernels for 21%

profile of v1, /device:TPU:1, one launch (start us, length us, event | category | flops | bytes accessed | tf_op | source)
XLA Modules:
  0.0 114.5 jit_solution(13381796250709831228)
XLA Ops:
  0.0 1.6 %copy-done.2 = bf16[2048,512]{1,0:T(8,128)(2,1)S(1)} copy-done((bf16[2048,512]{1,0:T(8,128)(2,1)S(1)}, bf16[2048,512]{1,0:T(8,128)(2,1)}, u32[]{:S(2)}) %copy-start.2) | copy-done | bytes 2097176
  1.6 0.9 copy-done.6
  2.5 0.5 queries.1
  3.0 2.2 %collective-permute-start = (bf16[32,512]{1,0:T(8,128)(2,1)S(1)}, bf16[32,512]{1,0:T(8,128)(2,1)S(1)}, u32[]{:S(2)}, u32[]{:S(2)}) collective-permute-start(bf16[32,512]{1,0:T(8,128)(2,1)S(1)} %queries.1), channel_id=1, source_target_pairs={{0,4},{4,0},{1,5},{5,1},{2,6},{6,2},{3,7},{7,3},{8,12},{12,8},{9,1... | collective-permute-start | bytes 98312 | tf_op jit(solution)/shard_map/ppermute | solution.py:328
  5.5 1.0 collective-permute-done
  6.6 2.7 %collective-permute-start.3 = (bf16[64,512]{1,0:T(8,128)(2,1)S(1)}, bf16[64,512]{1,0:T(8,128)(2,1)S(1)}, u32[]{:S(2)}, u32[]{:S(2)}) collective-permute-start(bf16[64,512]{1,0:T(8,128)(2,1)S(1)} %maximum_select_fusion.1.after_ref), channel_id=1, source_target_pairs={{0,24},{1,97},{8,0},{9,105},{16,8},{17,113},{24,16},{25,121},{32,5... | collective-permute-start | bytes 196616 | tf_op jit(solution)/shard_map/ppermute | solution.py:345
  9.3 0.5 collective-permute-start.2
  9.8 0.6 collective-permute-start.1
  10.4 3.4 %copy-done.8 = bf16[2048,2048]{1,0:T(8,128)(2,1)S(1)} copy-done((bf16[2048,2048]{1,0:T(8,128)(2,1)S(1)}, bf16[2048,2048]{1,0:T(8,128)(2,1)}, u32[]{:S(2)}) %copy-start.8) | copy-done | bytes 8388632
  13.8 5.1 %keys.1.k_ref = bf16[2048,512]{1,0:T(8,128)(2,1)S(1)} custom-call(bf16[2048,2048]{1,0:T(8,128)(2,1)S(1)} %copy-done.8, bf16[2048,512]{1,0:T(8,128)(2,1)S(1)} %copy-done.9, bf16[64,512]{1,0:T(8,128)(2,1)S(1)} %maximum_select_fusion.1.after_ref), custom_call_target="tpu_custom_call" | custom-call | flops 4294967296 | bytes 10485760 | tf_op jit(solution)/shard_map/keys/pallas_call | solution.py:81
  19.0 1.7 %collective-permute-start.8 = (bf16[256,512]{1,0:T(8,128)(2,1)S(1)}, bf16[256,512]{1,0:T(8,128)(2,1)S(1)}, u32[]{:S(2)}, u32[]{:S(2)}) collective-permute-start(bf16[256,512]{1,0:T(8,128)(2,1)S(1)} %pad_maximum_fusion.1.after_ref.q_ref), channel_id=1, source_target_pairs={{0,32},{1,9},{8,40},{9,17},{16,48},{17,25},{24,56},{25,1},{32,64},... | collective-permute-start | bytes 786440 | tf_op jit(solution)/shard_map/ppermute | solution.py:345
  20.7 2.2 %collective-permute-start.6 = (bf16[256,512]{1,0:T(8,128)(2,1)S(1)}, bf16[256,512]{1,0:T(8,128)(2,1)S(1)}, u32[]{:S(2)}, u32[]{:S(2)}) collective-permute-start(bf16[256,512]{1,0:T(8,128)(2,1)S(1)} %pad_maximum_fusion.1.after_ref.q_ref), channel_id=1, source_target_pairs={{0,96},{1,25},{8,104},{9,1},{16,112},{17,9},{24,120},{25,17},{32,0... | collective-permute-start | bytes 786440 | tf_op jit(solution)/shard_map/ppermute | solution.py:345
  23.0 1.2 %collective-permute-start.4 = (bf16[256,512]{1,0:T(8,128)(2,1)S(1)}, bf16[256,512]{1,0:T(8,128)(2,1)S(1)}, u32[]{:S(2)}, u32[]{:S(2)}) collective-permute-start(bf16[256,512]{1,0:T(8,128)(2,1)S(1)} %pad_maximum_fusion.1.after_ref.q_ref), channel_id=1, source_target_pairs={{0,64},{1,17},{8,72},{9,25},{16,80},{17,1},{24,88},{25,9},{32,96},... | collective-permute-start | bytes 786440 | tf_op jit(solution)/shard_map/ppermute | solution.py:345
  24.2 5.1 %values.1.v_ref = bf16[2048,512]{1,0:T(8,128)(2,1)S(1)} custom-call(bf16[2048,2048]{1,0:T(8,128)(2,1)S(1)} %copy-done.8, bf16[2048,512]{1,0:T(8,128)(2,1)S(1)} %copy-done.10, bf16[256,512]{1,0:T(8,128)(2,1)S(1)} %pad_maximum_fusion.1.after_ref.q_ref), custom_call_target="tpu_custom_call" | custom-call | flops 4294967296 | bytes 10485760 | tf_op jit(solution)/shard_map/values/pallas_call | solution.py:81
  29.2 1.7 %collective-permute-done.4.q_ref = bf16[256,512]{1,0:T(8,128)(2,1)S(1)} collective-permute-done((bf16[256,512]{1,0:T(8,128)(2,1)S(1)}, bf16[256,512]{1,0:T(8,128)(2,1)S(1)}, u32[]{:S(2)}, u32[]{:S(2)}) %collective-permute-start.4) | collective-permute-done | bytes 262176 | tf_op jit(solution)/shard_map/ppermute | solution.py:345
  31.1 3.3 %cross.4 = bf16[256,640]{1,0:T(8,128)(2,1)S(1)} custom-call(s32[6]{0:T(128)S(1)} %stack.55.ids_ref, s32[1024]{0:T(1024)S(1)} %broadcast_select_fusion.cutoff_ref, bf16[256,512]{1,0:T(8,128)(2,1)S(1)} %collective-permute-done.4.q_ref, bf16[2048,512]{1,0:T(8,128)(2,1)S(1)} %keys.1.k_ref, bf16[2048,512]{1,0:T(8,128)(2,1)S(1)} %values.1.v_ref, ...), custom_call_target="tpu_custom_call" | custom-call | flops 2147483648 | bytes 4194304 | tf_op jit(solution)/shard_map/cross/pallas_call | solution.py:173
  34.5 0.8 collective-permute-start.5
  35.2 3.5 %cross.5 = bf16[256,640]{1,0:T(8,128)(2,1)S(1)} custom-call(s32[6]{0:T(128)S(1)} %stack.55.ids_ref, s32[1024]{0:T(1024)S(1)} %broadcast_select_fusion.cutoff_ref, bf16[256,512]{1,0:T(8,128)(2,1)S(1)} %collective-permute-done.6.q_ref, bf16[2048,512]{1,0:T(8,128)(2,1)S(1)} %keys.1.k_ref, bf16[2048,512]{1,0:T(8,128)(2,1)S(1)} %values.1.v_ref, ...), custom_call_target="tpu_custom_call" | custom-call | flops 2147483648 | bytes 4194304 | tf_op jit(solution)/shard_map/cross/pallas_call | solution.py:173
  38.7 0.9 collective-permute-start.7
  39.6 3.3 %cross.6 = bf16[256,640]{1,0:T(8,128)(2,1)S(1)} custom-call(s32[6]{0:T(128)S(1)} %stack.55.ids_ref, s32[1024]{0:T(1024)S(1)} %broadcast_select_fusion.cutoff_ref, bf16[256,512]{1,0:T(8,128)(2,1)S(1)} %collective-permute-done.8.q_ref, bf16[2048,512]{1,0:T(8,128)(2,1)S(1)} %keys.1.k_ref, bf16[2048,512]{1,0:T(8,128)(2,1)S(1)} %values.1.v_ref, ...), custom_call_target="tpu_custom_call" | custom-call | flops 2147483648 | bytes 4194304 | tf_op jit(solution)/shard_map/cross/pallas_call | solution.py:173
  43.0 2.9 %collective-permute-start.9 = (bf16[256,640]{1,0:T(8,128)(2,1)S(1)}, bf16[256,640]{1,0:T(8,128)(2,1)S(1)}, u32[]{:S(2)}, u32[]{:S(2)}) collective-permute-start(bf16[256,640]{1,0:T(8,128)(2,1)S(1)} %cross.6), channel_id=1, source_target_pairs={{0,96},{1,25},{8,104},{9,1},{16,112},{17,9},{24,120},{25,17},{32,0... | collective-permute-start | bytes 983048 | tf_op jit(solution)/shard_map/ppermute | solution.py:345
  45.8 3.7 %cross.7.d_ref = bf16[256,640]{1,0:T(8,128)(2,1)S(1)} custom-call(s32[6]{0:T(128)S(1)} %stack.55.ids_ref, s32[1024]{0:T(1024)S(1)} %broadcast_select_fusion.cutoff_ref, bf16[256,512]{1,0:T(8,128)(2,1)S(1)} %pad_maximum_fusion.1.after_ref.q_ref, bf16[2048,512]{1,0:T(8,128)(2,1)S(1)} %keys.1.k_ref, bf16[2048,512]{1,0:T(8,128)(2,1)S(1)} %values.1.v_ref, ...), custom_call_target="tpu_custom_call" | custom-call | flops 2147483648 | bytes 4194304 | tf_op jit(solution)/shard_map/cross/pallas_call | solution.py:173
  49.6 0.2 collective-permute-done.9.c_ref
  49.9 1.0 blend.1
  50.9 11.0 %all_to_all.10.parts_ref = bf16[8,32,640]{2,1,0:T(8,128)(2,1)S(1)} all-to-all(bf16[8,32,640]{2,1,0:T(8,128)(2,1)S(1)} %bitcast.21), channel_id=1, replica_groups={{0,4,8,12,16,20,24,28},{1,5,33,37,65,69,97,101},{32,36,40,44,48,52,56,6..., dimensions={0} | all-to-all | bytes 655360 | tf_op jit(solution)/shard_map/all_to_all | solution.py:355
  61.9 0.7 cross_output.1
  62.6 4.8 %collective-permute-start.10 = (bf16[32,2048]{1,0:T(8,128)(2,1)S(1)}, bf16[32,2048]{1,0:T(8,128)(2,1)S(1)}, u32[]{:S(2)}, u32[]{:S(2)}) collective-permute-start(bf16[32,2048]{1,0:T(8,128)(2,1)S(1)} %cross_output.1), channel_id=1, source_target_pairs={{0,1},{1,0},{2,3},{3,2},{4,5},{5,4},{6,7},{7,6},{8,9},{9,8},{10,11... | collective-permute-start | bytes 393224 | tf_op jit(solution)/shard_map/ppermute | solution.py:328
  67.5 1.0 collective-permute-done.10
  68.5 2.7 %collective-permute-start.11 = (bf16[32,2048]{1,0:T(8,128)(2,1)S(1)}, bf16[32,2048]{1,0:T(8,128)(2,1)S(1)}, u32[]{:S(2)}, u32[]{:S(2)}) collective-permute-start(bf16[32,2048]{1,0:T(8,128)(2,1)S(1)} %add_convert_fusion.2.one_ref), channel_id=1, source_target_pairs={{0,2},{2,0},{1,3},{3,1},{4,6},{6,4},{5,7},{7,5},{8,10},{10,8},{9,1... | collective-permute-start | bytes 393224 | tf_op jit(solution)/shard_map/ppermute | solution.py:328
  71.2 3.6 %collective-permute-done.11.two_ref = bf16[32,2048]{1,0:T(8,128)(2,1)S(1)} collective-permute-done((bf16[32,2048]{1,0:T(8,128)(2,1)S(1)}, bf16[32,2048]{1,0:T(8,128)(2,1)S(1)}, u32[]{:S(2)}, u32[]{:S(2)}) %collective-permute-start.11) | collective-permute-done | bytes 131104 | tf_op jit(solution)/shard_map/ppermute | solution.py:328
  74.8 1.8 %self_project.1 = (f32[32,2048]{1,0:T(8,128)S(1)}, bf16[32,384]{1,0:T(8,128)(2,1)S(1)}, bf16[32,384]{1,0:T(8,128)(2,1)S(1)}, bf16[32,384]{1,0:T(8,128)(2,1)S(1)}, bf16[32,384]{1,0:T(8,128)(2,1)S(1)}) custom-call(s32[6]{0:T(128)S(1)} %stack.55.ids_ref, bf16[32,2048]{1,0:T(8,128)(2,1)S(1)} %copy-done.7, bf16[32,2048]{1,0:T(8,128)(2,1)S(1)} %add_convert_fusion.2.one_ref, ...), custom_call_target="tpu_custom_call" | custom-call | tf_op jit(solution)/shard_map/self_project/pallas_call | solution.py:259
  76.7 0.4 collective-permute-start.12
  77.0 1.7 %collective-permute-start.13 = (bf16[32,384]{1,0:T(8,128)(2,1)S(1)}, bf16[32,384]{1,0:T(8,128)(2,1)S(1)}, u32[]{:S(2)}, u32[]{:S(2)}) collective-permute-start(bf16[32,384]{1,0:T(8,128)(2,1)S(1)} %get-tuple-element.17), channel_id=1, source_target_pairs={{0,64},{1,17},{8,72},{9,25},{16,80},{17,1},{24,88},{25,9},{32,96},... | collective-permute-start | bytes 73736 | tf_op jit(solution)/shard_map/ppermute | solution.py:345
  78.8 1.0 collective-permute-start.14
  79.8 0.8 collective-permute-done.12.b_ref
  80.6 0.6 collective-permute-done.13.c_ref
  81.5 9.6 %all_to_all.11.kv_ref = bf16[8,128,256]{2,1,0:T(8,128)(2,1)S(1)} all-to-all(bf16[8,128,256]{2,1,0:T(8,128)(2,1)S(1)} %broadcast_in_dim.5), channel_id=1, replica_groups={{0,4,8,12,16,20,24,28},{1,5,33,37,65,69,97,101},{32,36,40,44,48,52,56,6..., dimensions={0} | all-to-all | bytes 1048576 | tf_op jit(solution)/shard_map/all_to_all | solution.py:355
  91.1 1.1 %self_attend.1 = (bf16[32,128]{1,0:T(8,128)(2,1)S(1)}, bf16[32,128]{1,0:T(8,128)(2,1)S(1)}, bf16[32,128]{1,0:T(8,128)(2,1)S(1)}, bf16[32,128]{1,0:T(8,128)(2,1)S(1)}) custom-call(s32[6]{0:T(128)S(1)} %stack.55.ids_ref, bf16[32,384]{1,0:T(8,128)(2,1)S(1)} %get-tuple-element.15.a_ref, bf16[32,384]{1,0:T(8,128)(2,1)S(1)} %collective-permute-done.12.b_ref, ...), custom_call_target="tpu_custom_call" | custom-call | tf_op jit(solution)/shard_map/self_attend/pallas_call | solution.py:297
  92.3 3.0 %collective-permute-start.15 = (bf16[32,128]{1,0:T(8,128)(2,1)S(1)}, bf16[32,128]{1,0:T(8,128)(2,1)S(1)}, u32[]{:S(2)}, u32[]{:S(2)}) collective-permute-start(bf16[32,128]{1,0:T(8,128)(2,1)S(1)} %get-tuple-element.20), channel_id=1, source_target_pairs={{0,96},{1,25},{8,104},{9,1},{16,112},{17,9},{24,120},{25,17},{32,0... | collective-permute-start | bytes 24584 | tf_op jit(solution)/shard_map/ppermute | solution.py:345
  95.3 0.3 collective-permute-start.16
  95.6 0.3 collective-permute-start.17
  96.1 3.2 %collective-permute-done.16.c_ref = bf16[32,128]{1,0:T(8,128)(2,1)S(1)} collective-permute-done((bf16[32,128]{1,0:T(8,128)(2,1)S(1)}, bf16[32,128]{1,0:T(8,128)(2,1)S(1)}, u32[]{:S(2)}, u32[]{:S(2)}) %collective-permute-start.16) | collective-permute-done | bytes 8224 | tf_op jit(solution)/shard_map/ppermute | solution.py:345
  99.4 1.0 self_output.1
  100.4 6.1 %collective-permute-start.18 = (bf16[32,2048]{1,0:T(8,128)(2,1)S(1)}, bf16[32,2048]{1,0:T(8,128)(2,1)S(1)}, u32[]{:S(2)}, u32[]{:S(2)}) collective-permute-start(bf16[32,2048]{1,0:T(8,128)(2,1)S(1)} %self_output.1), channel_id=1, source_target_pairs={{0,1},{1,0},{2,3},{3,2},{4,5},{5,4},{6,7},{7,6},{8,9},{9,8},{10,11... | collective-permute-start | bytes 393224 | tf_op jit(solution)/shard_map/ppermute | solution.py:328
  106.4 1.0 collective-permute-done.18
  107.5 2.7 %collective-permute-start.19 = (bf16[32,2048]{1,0:T(8,128)(2,1)S(1)}, bf16[32,2048]{1,0:T(8,128)(2,1)S(1)}, u32[]{:S(2)}, u32[]{:S(2)}) collective-permute-start(bf16[32,2048]{1,0:T(8,128)(2,1)S(1)} %add_convert_fusion.1), channel_id=1, source_target_pairs={{0,2},{2,0},{1,3},{3,1},{4,6},{6,4},{5,7},{7,5},{8,10},{10,8},{9,1... | collective-permute-start | bytes 393224 | tf_op jit(solution)/shard_map/ppermute | solution.py:328
  110.2 3.6 %collective-permute-done.19 = bf16[32,2048]{1,0:T(8,128)(2,1)S(1)} collective-permute-done((bf16[32,2048]{1,0:T(8,128)(2,1)S(1)}, bf16[32,2048]{1,0:T(8,128)(2,1)S(1)}, u32[]{:S(2)}, u32[]{:S(2)}) %collective-permute-start.19) | collective-permute-done | bytes 131104 | tf_op jit(solution)/shard_map/ppermute | solution.py:328
  113.8 0.7 add_convert_fusion
  (50 shorter events, 1.2 us)
Async XLA Ops:
  0.0 1.6 %copy-start.2 = (bf16[2048,512]{1,0:T(8,128)(2,1)S(1)}, bf16[2048,512]{1,0:T(8,128)(2,1)}, u32[]{:S(2)}) copy-start(bf16[2048,512]{1,0:T(8,128)(2,1)} %wq_ref.2) | copy-start | bytes 6291460
  1.6 0.9 copy-start.6
  2.5 2.7 %copy-start.11 = (s32[1024]{0:T(1024)S(1)}, s32[1024]{0:T(1024)}, u32[]{:S(2)}) copy-start(s32[1024]{0:T(1024)} %param.13) | copy-start | bytes 12292
  2.5 7.9 %copy-start.9 = (bf16[2048,512]{1,0:T(8,128)(2,1)S(1)}, bf16[2048,512]{1,0:T(8,128)(2,1)}, u32[]{:S(2)}) copy-start(bf16[2048,512]{1,0:T(8,128)(2,1)} %w_ref.2) | copy-start | bytes 6291460
  3.0 3.5 %collective-permute-start = (bf16[32,512]{1,0:T(8,128)(2,1)S(1)}, bf16[32,512]{1,0:T(8,128)(2,1)S(1)}, u32[]{:S(2)}, u32[]{:S(2)}) collective-permute-start(bf16[32,512]{1,0:T(8,128)(2,1)S(1)} %queries.1), channel_id=1, source_target_pairs={{0,4},{4,0},{1,5},{5,1},{2,6},{6,2},{3,7},{7,3},{8,12},{12,8},{9,1... | collective-permute-start | bytes 98312 | tf_op jit(solution)/shard_map/ppermute | solution.py:328
  6.6 12.3 %collective-permute-start.3 = (bf16[64,512]{1,0:T(8,128)(2,1)S(1)}, bf16[64,512]{1,0:T(8,128)(2,1)S(1)}, u32[]{:S(2)}, u32[]{:S(2)}) collective-permute-start(bf16[64,512]{1,0:T(8,128)(2,1)S(1)} %maximum_select_fusion.1.after_ref), channel_id=1, source_target_pairs={{0,24},{1,97},{8,0},{9,105},{16,8},{17,113},{24,16},{25,121},{32,5... | collective-permute-start | bytes 196616 | tf_op jit(solution)/shard_map/ppermute | solution.py:345
  9.3 9.6 %collective-permute-start.2 = (bf16[64,512]{1,0:T(8,128)(2,1)S(1)}, bf16[64,512]{1,0:T(8,128)(2,1)S(1)}, u32[]{:S(2)}, u32[]{:S(2)}) collective-permute-start(bf16[64,512]{1,0:T(8,128)(2,1)S(1)} %maximum_select_fusion.1.after_ref), channel_id=1, source_target_pairs={{0,16},{1,65},{8,24},{9,73},{16,0},{17,81},{24,8},{25,89},{32,48},... | collective-permute-start | bytes 196616 | tf_op jit(solution)/shard_map/ppermute | solution.py:345
  9.8 9.1 %collective-permute-start.1 = (bf16[64,512]{1,0:T(8,128)(2,1)S(1)}, bf16[64,512]{1,0:T(8,128)(2,1)S(1)}, u32[]{:S(2)}, u32[]{:S(2)}) collective-permute-start(bf16[64,512]{1,0:T(8,128)(2,1)S(1)} %maximum_select_fusion.1.after_ref), channel_id=1, source_target_pairs={{0,8},{1,33},{8,16},{9,41},{16,24},{17,49},{24,0},{25,57},{32,40},... | collective-permute-start | bytes 196616 | tf_op jit(solution)/shard_map/ppermute | solution.py:345
  10.4 3.4 %copy-start.8 = (bf16[2048,2048]{1,0:T(8,128)(2,1)S(1)}, bf16[2048,2048]{1,0:T(8,128)(2,1)}, u32[]{:S(2)}) copy-start(bf16[2048,2048]{1,0:T(8,128)(2,1)} %context_ref.3) | copy-start | bytes 25165828
  13.8 10.4 %copy-start.10 = (bf16[2048,512]{1,0:T(8,128)(2,1)S(1)}, bf16[2048,512]{1,0:T(8,128)(2,1)}, u32[]{:S(2)}) copy-start(bf16[2048,512]{1,0:T(8,128)(2,1)} %w_ref.3) | copy-start | bytes 6291460
  19.0 20.6 %collective-permute-start.8 = (bf16[256,512]{1,0:T(8,128)(2,1)S(1)}, bf16[256,512]{1,0:T(8,128)(2,1)S(1)}, u32[]{:S(2)}, u32[]{:S(2)}) collective-permute-start(bf16[256,512]{1,0:T(8,128)(2,1)S(1)} %pad_maximum_fusion.1.after_ref.q_ref), channel_id=1, source_target_pairs={{0,32},{1,9},{8,40},{9,17},{16,48},{17,25},{24,56},{25,1},{32,64},... | collective-permute-start | bytes 786440 | tf_op jit(solution)/shard_map/ppermute | solution.py:345
  20.7 14.5 %collective-permute-start.6 = (bf16[256,512]{1,0:T(8,128)(2,1)S(1)}, bf16[256,512]{1,0:T(8,128)(2,1)S(1)}, u32[]{:S(2)}, u32[]{:S(2)}) collective-permute-start(bf16[256,512]{1,0:T(8,128)(2,1)S(1)} %pad_maximum_fusion.1.after_ref.q_ref), channel_id=1, source_target_pairs={{0,96},{1,25},{8,104},{9,1},{16,112},{17,9},{24,120},{25,17},{32,0... | collective-permute-start | bytes 786440 | tf_op jit(solution)/shard_map/ppermute | solution.py:345
  23.0 8.0 %collective-permute-start.4 = (bf16[256,512]{1,0:T(8,128)(2,1)S(1)}, bf16[256,512]{1,0:T(8,128)(2,1)S(1)}, u32[]{:S(2)}, u32[]{:S(2)}) collective-permute-start(bf16[256,512]{1,0:T(8,128)(2,1)S(1)} %pad_maximum_fusion.1.after_ref.q_ref), channel_id=1, source_target_pairs={{0,64},{1,17},{8,72},{9,25},{16,80},{17,1},{24,88},{25,9},{32,96},... | collective-permute-start | bytes 786440 | tf_op jit(solution)/shard_map/ppermute | solution.py:345
  34.5 15.2 %collective-permute-start.5 = (bf16[256,640]{1,0:T(8,128)(2,1)S(1)}, bf16[256,640]{1,0:T(8,128)(2,1)S(1)}, u32[]{:S(2)}, u32[]{:S(2)}) collective-permute-start(bf16[256,640]{1,0:T(8,128)(2,1)S(1)} %cross.4), channel_id=1, source_target_pairs={{0,64},{1,17},{8,72},{9,25},{16,80},{17,1},{24,88},{25,9},{32,96},... | collective-permute-start | bytes 983048 | tf_op jit(solution)/shard_map/ppermute | solution.py:345
  38.7 10.9 %collective-permute-start.7 = (bf16[256,640]{1,0:T(8,128)(2,1)S(1)}, bf16[256,640]{1,0:T(8,128)(2,1)S(1)}, u32[]{:S(2)}, u32[]{:S(2)}) collective-permute-start(bf16[256,640]{1,0:T(8,128)(2,1)S(1)} %cross.5), channel_id=1, source_target_pairs={{0,32},{1,9},{8,40},{9,17},{16,48},{17,25},{24,56},{25,1},{32,64},... | collective-permute-start | bytes 983048 | tf_op jit(solution)/shard_map/ppermute | solution.py:345
  43.0 6.9 %collective-permute-start.9 = (bf16[256,640]{1,0:T(8,128)(2,1)S(1)}, bf16[256,640]{1,0:T(8,128)(2,1)S(1)}, u32[]{:S(2)}, u32[]{:S(2)}) collective-permute-start(bf16[256,640]{1,0:T(8,128)(2,1)S(1)} %cross.6), channel_id=1, source_target_pairs={{0,96},{1,25},{8,104},{9,1},{16,112},{17,9},{24,120},{25,17},{32,0... | collective-permute-start | bytes 983048 | tf_op jit(solution)/shard_map/ppermute | solution.py:345
  45.8 28.9 %copy-start.4 = (bf16[2048,512]{1,0:T(8,128)(2,1)S(1)}, bf16[2048,512]{1,0:T(8,128)(2,1)}, u32[]{:S(2)}) copy-start(bf16[2048,512]{1,0:T(8,128)(2,1)} %wk_ref.1) | copy-start | bytes 6291460
  45.8 28.9 %copy-start.5 = (bf16[2048,512]{1,0:T(8,128)(2,1)S(1)}, bf16[2048,512]{1,0:T(8,128)(2,1)}, u32[]{:S(2)}) copy-start(bf16[2048,512]{1,0:T(8,128)(2,1)} %wv_ref.1) | copy-start | bytes 6291460
  49.6 12.3 %copy-start = (bf16[512,2048]{1,0:T(8,128)(2,1)S(1)}, bf16[512,2048]{1,0:T(8,128)(2,1)}, u32[]{:S(2)}) copy-start(bf16[512,2048]{1,0:T(8,128)(2,1)} %wo_ref.2) | copy-start | bytes 6291460
  50.8 23.9 %copy-start.3 = (bf16[2048,512]{1,0:T(8,128)(2,1)S(1)}, bf16[2048,512]{1,0:T(8,128)(2,1)}, u32[]{:S(2)}) copy-start(bf16[2048,512]{1,0:T(8,128)(2,1)} %wq_ref.3) | copy-start | bytes 6291460
  50.9 23.9 %copy-start.7 = (bf16[32,2048]{1,0:T(8,128)(2,1)S(1)}, bf16[32,2048]{1,0:T(8,128)(2,1)}, u32[]{:S(2)}) copy-start(bf16[32,2048]{1,0:T(8,128)(2,1)} %latent_ref.3) | copy-start | bytes 393220
  62.6 5.8 %collective-permute-start.10 = (bf16[32,2048]{1,0:T(8,128)(2,1)S(1)}, bf16[32,2048]{1,0:T(8,128)(2,1)S(1)}, u32[]{:S(2)}, u32[]{:S(2)}) collective-permute-start(bf16[32,2048]{1,0:T(8,128)(2,1)S(1)} %cross_output.1), channel_id=1, source_target_pairs={{0,1},{1,0},{2,3},{3,2},{4,5},{5,4},{6,7},{7,6},{8,9},{9,8},{10,11... | collective-permute-start | bytes 393224 | tf_op jit(solution)/shard_map/ppermute | solution.py:328
  68.5 6.3 %collective-permute-start.11 = (bf16[32,2048]{1,0:T(8,128)(2,1)S(1)}, bf16[32,2048]{1,0:T(8,128)(2,1)S(1)}, u32[]{:S(2)}, u32[]{:S(2)}) collective-permute-start(bf16[32,2048]{1,0:T(8,128)(2,1)S(1)} %add_convert_fusion.2.one_ref), channel_id=1, source_target_pairs={{0,2},{2,0},{1,3},{3,1},{4,6},{6,4},{5,7},{7,5},{8,10},{10,8},{9,1... | collective-permute-start | bytes 393224 | tf_op jit(solution)/shard_map/ppermute | solution.py:328
  76.7 22.7 %copy-start.1 = (bf16[512,2048]{1,0:T(8,128)(2,1)S(1)}, bf16[512,2048]{1,0:T(8,128)(2,1)}, u32[]{:S(2)}) copy-start(bf16[512,2048]{1,0:T(8,128)(2,1)} %wo_ref.3) | copy-start | bytes 6291460
  76.7 4.0 %collective-permute-start.12 = (bf16[32,384]{1,0:T(8,128)(2,1)S(1)}, bf16[32,384]{1,0:T(8,128)(2,1)S(1)}, u32[]{:S(2)}, u32[]{:S(2)}) collective-permute-start(bf16[32,384]{1,0:T(8,128)(2,1)S(1)} %get-tuple-element.16), channel_id=1, source_target_pairs={{0,32},{1,9},{8,40},{9,17},{16,48},{17,25},{24,56},{25,1},{32,64},... | collective-permute-start | bytes 73736 | tf_op jit(solution)/shard_map/ppermute | solution.py:345
  77.0 4.2 %collective-permute-start.13 = (bf16[32,384]{1,0:T(8,128)(2,1)S(1)}, bf16[32,384]{1,0:T(8,128)(2,1)S(1)}, u32[]{:S(2)}, u32[]{:S(2)}) collective-permute-start(bf16[32,384]{1,0:T(8,128)(2,1)S(1)} %get-tuple-element.17), channel_id=1, source_target_pairs={{0,64},{1,17},{8,72},{9,25},{16,80},{17,1},{24,88},{25,9},{32,96},... | collective-permute-start | bytes 73736 | tf_op jit(solution)/shard_map/ppermute | solution.py:345
  78.8 2.7 %collective-permute-start.14 = (bf16[32,384]{1,0:T(8,128)(2,1)S(1)}, bf16[32,384]{1,0:T(8,128)(2,1)S(1)}, u32[]{:S(2)}, u32[]{:S(2)}) collective-permute-start(bf16[32,384]{1,0:T(8,128)(2,1)S(1)} %get-tuple-element.18), channel_id=1, source_target_pairs={{0,96},{1,25},{8,104},{9,1},{16,112},{17,9},{24,120},{25,17},{32,0... | collective-permute-start | bytes 73736 | tf_op jit(solution)/shard_map/ppermute | solution.py:345
  92.3 3.8 %collective-permute-start.15 = (bf16[32,128]{1,0:T(8,128)(2,1)S(1)}, bf16[32,128]{1,0:T(8,128)(2,1)S(1)}, u32[]{:S(2)}, u32[]{:S(2)}) collective-permute-start(bf16[32,128]{1,0:T(8,128)(2,1)S(1)} %get-tuple-element.20), channel_id=1, source_target_pairs={{0,96},{1,25},{8,104},{9,1},{16,112},{17,9},{24,120},{25,17},{32,0... | collective-permute-start | bytes 24584 | tf_op jit(solution)/shard_map/ppermute | solution.py:345
  95.3 4.0 %collective-permute-start.16 = (bf16[32,128]{1,0:T(8,128)(2,1)S(1)}, bf16[32,128]{1,0:T(8,128)(2,1)S(1)}, u32[]{:S(2)}, u32[]{:S(2)}) collective-permute-start(bf16[32,128]{1,0:T(8,128)(2,1)S(1)} %get-tuple-element.21), channel_id=1, source_target_pairs={{0,64},{1,17},{8,72},{9,25},{16,80},{17,1},{24,88},{25,9},{32,96},... | collective-permute-start | bytes 24584 | tf_op jit(solution)/shard_map/ppermute | solution.py:345
  95.6 3.7 %collective-permute-start.17 = (bf16[32,128]{1,0:T(8,128)(2,1)S(1)}, bf16[32,128]{1,0:T(8,128)(2,1)S(1)}, u32[]{:S(2)}, u32[]{:S(2)}) collective-permute-start(bf16[32,128]{1,0:T(8,128)(2,1)S(1)} %get-tuple-element.22), channel_id=1, source_target_pairs={{0,32},{1,9},{8,40},{9,17},{16,48},{17,25},{24,56},{25,1},{32,64},... | collective-permute-start | bytes 24584 | tf_op jit(solution)/shard_map/ppermute | solution.py:345
  100.4 7.0 %collective-permute-start.18 = (bf16[32,2048]{1,0:T(8,128)(2,1)S(1)}, bf16[32,2048]{1,0:T(8,128)(2,1)S(1)}, u32[]{:S(2)}, u32[]{:S(2)}) collective-permute-start(bf16[32,2048]{1,0:T(8,128)(2,1)S(1)} %self_output.1), channel_id=1, source_target_pairs={{0,1},{1,0},{2,3},{3,2},{4,5},{5,4},{6,7},{7,6},{8,9},{9,8},{10,11... | collective-permute-start | bytes 393224 | tf_op jit(solution)/shard_map/ppermute | solution.py:328
  107.5 6.3 %collective-permute-start.19 = (bf16[32,2048]{1,0:T(8,128)(2,1)S(1)}, bf16[32,2048]{1,0:T(8,128)(2,1)S(1)}, u32[]{:S(2)}, u32[]{:S(2)}) collective-permute-start(bf16[32,2048]{1,0:T(8,128)(2,1)S(1)} %add_convert_fusion.1), channel_id=1, source_target_pairs={{0,2},{2,0},{1,3},{3,1},{4,6},{6,4},{5,7},{7,5},{8,10},{10,8},{9,1... | collective-permute-start | bytes 393224 | tf_op jit(solution)/shard_map/ppermute | solution.py:328
